TPU v7x, 32 devices: a whole 2x2x4 slice. The times are simulated.
32 devices in a mesh: dp: 8 (over z, core), group: 4 (over y, x).
Axes of the slice: x: 2, y: 2, z: 4, core: 2. Of those that a mesh axis runs over, the one named last changes fastest.
Arguments:
- layer_input: bfloat16 [2048, 8192], P('dp', 'group'), may hold values from -30 to 30
- kv_cotangent: bfloat16 [2048, 2048], P('dp', 'group'), may hold values from -70 to 70
- weight_codes: bfloat16 [2048, 8192], P('dp', 'group'), may hold values from -256 to 256
- block_scales: bfloat16 [2048, 32], P('dp', 'group'), may hold values from 0.00024986267 to 0.0009994507
- master: float32 [2048, 8192], P('dp', 'group'), may hold values from -6 to 6
- moment_one: float32 [2048, 8192], P('dp', 'group'), may hold values from -0.75 to 0.75
- moment_two: float32 [2048, 8192], P('dp', 'group'), may hold values from 0.001 to 0.01
Outputs:
- grad_input: bfloat16 [2048, 8192], P('dp', 'group')
- new_master: float32 [2048, 8192], P('dp', 'group')
- new_moment_one: float32 [2048, 8192], P('dp', 'group')
- new_moment_two: float32 [2048, 8192], P('dp', 'group')
All inputs are finite; a program needn't handle non-finite values.
Results may differ from a plain program's by a relative error of at most 0.0049.
Values may be sent and summed in bfloat16 or wider, within the bound.
A program may use at most 128 MiB of HBM per device.

v0:
```python
import functools
import jax
import jax.numpy as jnp
from jax import lax
from jax.experimental import pallas as pl
from jax.experimental.pallas import tpu as pltpu
from jax.sharding import PartitionSpec as P

BLOCK = 256
CLIP = 2048


BETA_ONE = 0.9
BETA_TWO = 0.95
LEARN_RATE = 0.25
DECAY_RATE = 0.1
EPS_ADAM = 1e-08
EPS_NORM = 1e-06

MESH = pl.DeviceIdType.MESH
PIECES = 4
DEPTH = 3


def dequantize(codes, scales):
    row_count, col_count = codes.shape
    blocked = (
        codes.astype(jnp.float32).reshape(row_count, col_count // BLOCK, BLOCK)
        * scales.astype(jnp.float32)[:, :, None]
    )
    return blocked.reshape(row_count, col_count).astype(jnp.bfloat16)


def adamw(clipped, master, moment_one, moment_two):
    new_moment_one = BETA_ONE * moment_one + (1.0 - BETA_ONE) * clipped
    new_moment_two = BETA_TWO * moment_two + (1.0 - BETA_TWO) * clipped * clipped
    first_fix = 1.0 - BETA_ONE**10
    second_fix = 1.0 - BETA_TWO**10
    update = new_moment_one / first_fix / (jnp.sqrt(new_moment_two / second_fix) + EPS_ADAM)
    new_master = master - LEARN_RATE * (update + DECAY_RATE * master)
    return new_master, new_moment_one, new_moment_two


def general(layer_input, kv_cotangent, weight_codes, block_scales, master, moment_one, moment_two):
    cot_whole = lax.all_gather(kv_cotangent, "group", axis=1, tiled=True)
    weight_piece = dequantize(
        lax.all_gather(weight_codes, "dp", axis=0, tiled=True),
        lax.all_gather(block_scales, "dp", axis=0, tiled=True),
    )
    grad_input = jnp.dot(
        cot_whole, weight_piece, preferred_element_type=jnp.float32
    ).astype(jnp.bfloat16)
    partial_value = jnp.einsum(
        "tc,td->cd", cot_whole, layer_input, preferred_element_type=jnp.float32
    )
    gradient = lax.psum_scatter(
        lax.optimization_barrier(partial_value.astype(jnp.bfloat16)).astype(jnp.float32),
        "dp",
        scatter_dimension=0,
        tiled=True,
    )
    square_total = lax.psum(jnp.sum(gradient * gradient), ("dp", "group"))
    factor = jnp.minimum(1.0, CLIP / (jnp.sqrt(square_total) + EPS_NORM))
    return (grad_input,) + adamw(gradient * factor, master, moment_one, moment_two)


def kernel(
    Z, G, cot_ref, li_ref, codes_ref, scales_ref, gi_ref, g_ref,
    codes, scales_in, cotp, lip, wbuf, rbuf, facc, gsib, near, far, local,
    line_send, line_recv, sib_send, sib_recv, cot_send, cot_recv, csib_send, csib_recv,
    li_send, li_recv, fin_send, fin_recv, near_send, near_recv, far_send, far_recv,
):
    K = PIECES
    tok, head = cot_ref.shape
    feat, cols = codes_ref.shape
    half = cols // 2
    unit = 2 * feat
    g_rows, r_rows = feat // K, unit // K

    dp, g = lax.axis_index("dp"), lax.axis_index("group")
    z = lax.div(dp, 2)
    c = dp - 2 * z
    sibling = (2 * z + 1 - c, g)

    def plane(j):
        place = lax.rem(c * G + g + j, 2 * G)
        core = lax.div(place, G)
        return (2 * z + core, place - core * G)

    def line(j):
        return (2 * lax.rem(z + j, Z) + c, g)

    barrier = pltpu.get_barrier_semaphore()
    for j in range(1, 2 * G):
        pl.semaphore_signal(barrier, inc=1, device_id=plane(j), device_id_type=MESH)
    for j in range(1, Z):
        pl.semaphore_signal(barrier, inc=1, device_id=line(j), device_id_type=MESH)

    fetch_codes = pltpu.make_async_copy(codes_ref, codes, local.at[2])
    fetch_scales = pltpu.make_async_copy(scales_ref, scales_in, local.at[3])
    fetch_codes.start()
    fetch_scales.start()
    own_tok = pl.ds(pl.multiple_of(c * tok, tok), tok)
    fetch_li = pltpu.make_async_copy(
        li_ref.at[:, pl.ds(pl.multiple_of(c * half, half), half)], lip.at[own_tok, :], local.at[0])
    fetch_cot = pltpu.make_async_copy(
        cot_ref, cotp.at[own_tok, pl.ds(pl.multiple_of(g * head, head), head)], local.at[1])
    fetch_li.start()
    fetch_cot.start()

    own = pl.multiple_of(dp * feat, feat)
    fetch_scales.wait()
    scales = scales_in[...].astype(jnp.float32).T
    fetch_codes.wait()
    for j in range(cols // BLOCK):
        wbuf[pl.ds(own, feat), j * BLOCK:(j + 1) * BLOCK] = (
            codes[:, j * BLOCK:(j + 1) * BLOCK].astype(jnp.float32) * scales[:, j:j + 1]
        ).astype(jnp.bfloat16)

    pl.semaphore_wait(barrier, 2 * G - 1 + Z - 1)

    def remote(src, dst, send, recv, device):
        return pltpu.make_async_remote_copy(
            src_ref=src, dst_ref=dst, send_sem=send, recv_sem=recv,
            device_id=device, device_id_type=MESH,
        )

    def cot_block(owner, core):
        return cotp.at[
            pl.ds(pl.multiple_of(core * tok, tok), tok),
            pl.ds(pl.multiple_of(owner * head, head), head),
        ]

    def cot_copy(j, owner):
        return remote(cot_ref, cot_block(owner, c), cot_send.at[j - 1], cot_recv.at[j - 1],
                      (dp, lax.rem(g + j, G)))

    def cot_pass(j, core):
        owner = lax.rem(g + G - j, G)
        block = cot_block(owner, core)
        return remote(cot_ref if j == 0 else block, block, csib_send.at[j], csib_recv.at[j], sibling)

    for j in range(1, G):
        cot_copy(j, g).start()
    cot_pass(0, c).start()

    def li_copy(core, side):
        return remote(
            li_ref.at[:, pl.ds(pl.multiple_of(side * half, half), half)],
            lip.at[pl.ds(pl.multiple_of(core * tok, tok), tok), :],
            li_send.at[0], li_recv.at[0], sibling,
        )

    li_copy(c, 1 - c).start()

    places = (z, Z - 1 - z)
    nexts = ((dp + 2, g), (dp - 2, g))

    def true_z(way, q):
        return q if way == 0 else Z - 1 - q

    def weight_chunk(zz, core, k):
        return wbuf.at[pl.ds(pl.multiple_of((2 * zz + core) * feat + k * g_rows, g_rows), g_rows), :]

    def sum_chunk(way, dm, k):
        return rbuf.at[way, dm - 1, pl.ds(pl.multiple_of(k * r_rows, r_rows), r_rows), :]

    def line_copy(way, ref, step):
        return remote(ref, ref, line_send.at[way, step], line_recv.at[way, step], nexts[way])

    def sib_copy(zz, core, k):
        ref = weight_chunk(zz, core, k)
        return remote(ref, ref, sib_send.at[zz * K + k], sib_recv.at[zz * K + k], sibling)

    def partial_sum(zz, k):
        first = pl.multiple_of(zz * unit + k * r_rows, r_rows)
        return lax.dot_general(
            cotp[:, pl.ds(first, r_rows)], lip[...],
            (((0,), (0,)), ((), ())), preferred_element_type=jnp.float32,
        )

    def send(way, ref, step):
        @pl.when(step >= DEPTH)
        def _():
            line_copy(way, weight_chunk(z, c, 0), step - DEPTH).wait_send()
        line_copy(way, ref, step).start()

    def weight_step(way, s, k):
        p = places[way]

        @pl.when(s <= p)
        def _():
            zz = true_z(way, p - s)
            ref = weight_chunk(zz, c, k)

            @pl.when(s > 0)
            def _():
                line_copy(way, ref, (s - 1) * K + k).wait_recv()

            @pl.when((s > 0) if way else (s >= 0))
            def _():
                sib_copy(zz, c, k).start()

            @pl.when(p < Z - 1)
            def _():
                send(way, ref, s * K + k)

    def sum_step(way, s, k):
        p = places[way]

        @pl.when((s > p) & (p < Z - 1))
        def _():
            dm = Z + p - s
            ref = sum_chunk(way, dm, k)
            value = partial_sum(true_z(way, dm), k)

            @pl.when(p > 0)
            def _():
                line_copy(way, ref, (s - 1) * K + k).wait_recv()
                ref[...] = (ref[...].astype(jnp.float32) + value).astype(jnp.bfloat16)

            @pl.when(p == 0)
            def _():
                ref[...] = value.astype(jnp.bfloat16)

            send(way, ref, s * K + k)

    def first_unit(k, carry):
        for way in (0, 1):
            weight_step(way, 0, k)
        return carry

    lax.fori_loop(0, DEPTH, first_unit, 0)
    for j in range(1, G):
        cot_copy(j, lax.rem(g + G - j, G)).wait_recv()
        cot_pass(j, c).start()
    lax.fori_loop(DEPTH, K, first_unit, 0)
    fetch_li.wait()
    fetch_cot.wait()
    li_copy(1 - c, c).wait_recv()
    for j in range(G):
        cot_pass(j, 1 - c).wait_recv()

    def later_unit(i, carry):
        s = lax.div(i, K)
        k = i - s * K
        for way in (0, 1):
            weight_step(way, s, k)
        for way in (0, 1):
            sum_step(way, s, k)
        return carry

    lax.fori_loop(K, Z * K, later_unit, 0)

    def arrive(i, carry):
        zz = lax.div(i, K)
        sib_copy(zz, 1 - c, i - zz * K).wait_recv()
        return carry

    lax.fori_loop(0, Z * K, arrive, 0)

    def input_tile(j, carry):
        at = pl.ds(pl.multiple_of(j * BLOCK, BLOCK), BLOCK)
        gi_ref[:, at] = jnp.dot(
            cotp[pl.ds(pl.multiple_of(c * tok, tok), tok), :], wbuf[:, at],
            preferred_element_type=jnp.float32,
        ).astype(jnp.bfloat16)
        return carry

    lax.fori_loop(0, cols // BLOCK, input_tile, 0)

    def own_sum(k, carry):
        facc[pl.ds(pl.multiple_of(k * r_rows, r_rows), r_rows), :] = partial_sum(z, k)
        return carry

    lax.fori_loop(0, K, own_sum, 0)

    def fin_copy(k, m):
        return remote(
            facc.at[pl.ds(pl.multiple_of(k * r_rows, r_rows), r_rows), :],
            gsib.at[pl.ds(pl.multiple_of(m * r_rows, r_rows), r_rows), :],
            fin_send.at[m], fin_recv.at[m], sibling,
        )

    near[0] = jnp.zeros(near.shape[1:], jnp.float32)

    def finish(k, carry):
        at = pl.ds(pl.multiple_of(k * r_rows, r_rows), r_rows)
        for way in (0, 1):
            p = places[way]

            @pl.when(p > 0)
            def _():
                ref = sum_chunk(way, p, k)
                line_copy(way, ref, (Z - 1) * K + k).wait_recv()
                facc[at, :] += ref[...].astype(jnp.float32)

        core = lax.div(k, K // 2)

        @pl.when(core != c)
        def _():
            fin_copy(k, k - core * (K // 2)).start()

        value = facc[at, :]
        squares = value * value
        total = squares[0:8, :]
        for i in range(1, r_rows // 8):
            total = total + squares[i * 8:(i + 1) * 8, :]
        short = total[:, 0:128]
        for i in range(1, half // 128):
            short = short + total[:, i * 128:(i + 1) * 128]
        near[0] += short
        return carry

    lax.fori_loop(0, K, finish, 0)

    for j in range(1, 2 * G):
        remote(near.at[0], near.at[j], near_send.at[j - 1], near_recv.at[j - 1], plane(j)).start()
    for j in range(1, 2 * G):
        remote(near.at[0], near.at[j], near_send.at[j - 1], near_recv.at[j - 1], plane(j)).wait_recv()
    total = near[0]
    for j in range(1, 2 * G):
        total = total + near[j]
    far[0] = total
    for j in range(1, Z):
        remote(far.at[0], far.at[j], far_send.at[j - 1], far_recv.at[j - 1], line(j)).start()
    for j in range(1, Z):
        remote(far.at[0], far.at[j], far_send.at[j - 1], far_recv.at[j - 1], line(j)).wait_recv()
    total = far[0]
    for j in range(1, Z):
        total = total + far[j]
    square_total = jnp.sum(total, axis=(0, 1), keepdims=True)
    factor = jnp.minimum(1.0, CLIP / (jnp.sqrt(square_total) + EPS_NORM))

    g_ref[:, pl.ds(pl.multiple_of(c * half, half), half)] = (
        facc[pl.ds(pl.multiple_of(c * feat, feat), feat), :] * factor)
    for m in range(K // 2):
        fin_copy(m, m).wait_recv()
    g_ref[:, pl.ds(pl.multiple_of((1 - c) * half, half), half)] = gsib[...] * factor

    for j in range(1, G):
        cot_copy(j, g).wait_send()
    for j in range(G):
        cot_pass(j, c).wait_send()
    li_copy(c, 1 - c).wait_send()

    def sent(i, carry):
        zz = lax.div(i, K)
        sib_copy(zz, c, i - zz * K).wait_send()
        return carry

    lax.fori_loop(0, Z * K, sent, 0)
    for way in (0, 1):
        @pl.when(places[way] < Z - 1)
        def _():
            for step in range(Z * K - DEPTH, Z * K):
                line_copy(way, weight_chunk(z, c, 0), step).wait_send()
    for m in range(K // 2):
        fin_copy(m, m).wait_send()
    for j in range(1, 2 * G):
        remote(near.at[0], near.at[j], near_send.at[j - 1], near_recv.at[j - 1], plane(j)).wait_send()
    for j in range(1, Z):
        remote(far.at[0], far.at[j], far_send.at[j - 1], far_recv.at[j - 1], line(j)).wait_send()


def fused(Z, G, layer_input, kv_cotangent, weight_codes, block_scales, master, moment_one, moment_two):
    tok, head = kv_cotangent.shape
    feat, cols = weight_codes.shape
    half = cols // 2
    K = PIECES
    dma = pltpu.SemaphoreType.DMA
    vmem = pl.BlockSpec(memory_space=pltpu.VMEM)
    whole = pl.BlockSpec(memory_space=pl.ANY)
    grad_input, clipped = pl.pallas_call(
        functools.partial(kernel, Z, G),
        out_shape=(
            jax.ShapeDtypeStruct((tok, cols), jnp.bfloat16),
            jax.ShapeDtypeStruct((feat, cols), jnp.float32),
        ),
        in_specs=[whole] * 4,
        out_specs=(vmem, vmem),
        scratch_shapes=[
            pltpu.VMEM((feat, cols), jnp.bfloat16),
            pltpu.VMEM((cols // BLOCK, feat), jnp.bfloat16),
            pltpu.VMEM((2 * tok, G * head), jnp.bfloat16),
            pltpu.VMEM((2 * tok, half), jnp.bfloat16),
            pltpu.VMEM((2 * Z * feat, cols), jnp.bfloat16),
            pltpu.VMEM((2, Z - 1, 2 * feat, half), jnp.bfloat16),
            pltpu.VMEM((2 * feat, half), jnp.float32),
            pltpu.VMEM((feat, half), jnp.float32),
            pltpu.VMEM((2 * G, 8, 128), jnp.float32),
            pltpu.VMEM((Z, 8, 128), jnp.float32),
            dma((4,)),
            dma((2, Z * K)), dma((2, Z * K)),
            dma((Z * K,)), dma((Z * K,)),
            dma((G - 1,)), dma((G - 1,)),
            dma((G,)), dma((G,)),
            dma((1,)), dma((1,)),
            dma((K // 2,)), dma((K // 2,)),
            dma((2 * G - 1,)), dma((2 * G - 1,)),
            dma((Z - 1,)), dma((Z - 1,)),
        ],
        compiler_params=pltpu.CompilerParams(
            collective_id=0, has_side_effects=True, vmem_limit_bytes=48 * 1024 * 1024,
        ),
        cost_estimate=pl.CostEstimate(
            flops=4 * tok * G * head * cols, bytes_accessed=10 * tok * cols, transcendentals=0,
        ),
    )(*(
        pltpu.with_memory_space_constraint(x, pltpu.HBM)
        for x in (kv_cotangent, layer_input, weight_codes, block_scales.T)
    ))
    return (grad_input,) + adamw(clipped, master, moment_one, moment_two)


def solution(mesh):
    devices, groups = mesh.shape["dp"], mesh.shape["group"]

    def shards(*args):
        tok, head = args[1].shape
        feat, cols = args[2].shape
        if devices == 8 and groups == 4 and feat == 256 and tok == 256 and cols % 512 == 0 and head == 2 * feat:
            return fused(devices // 2, groups, *args)
        return general(*args)

    return jax.shard_map(
        shards,
        mesh=mesh,
        in_specs=(P("dp", "group"),) * 7,
        out_specs=(P("dp", "group"), P("dp", "group"), P("dp", "group"), P("dp", "group")),
        check_vma=False,
    )
```

profile of v0, /device:TPU:0, one launch (start us, length us, event | category | flops | bytes accessed | tf_op | source)
XLA Modules:
  0.0 111.3 jit_solution(14027251459768902589)
XLA Ops:
  0.6 0.0 copy-start
  0.6 0.0 copy-start.1
  0.7 0.0 copy-start.2
  0.7 105.6 %shard_map.102 = (bf16[256,2048]{1,0:T(8,128)(2,1)S(1)}, f32[256,2048]{1,0:T(8,128)S(1)}) custom-call(bf16[256,512]{1,0:T(8,128)(2,1)} %cot_ref.1, bf16[256,2048]{1,0:T(8,128)(2,1)} %li_ref.1, bf16[256,2048]{1,0:T(8,128)(2,1)} %codes_ref.1, bf16[8,256]{1,0:T(8,128)(2,1)} %bitcast.1), custom_call_target="tpu_custom_call" | custom-call | flops 4294967296 | bytes 5242880 | tf_op jit(solution)/shard_map/pallas_call | solution.py:374
  106.3 0.0 copy-done
  106.3 0.0 copy-done.1
  106.3 0.0 copy-done.2
  106.3 4.0 %multiply_subtract_fusion = (f32[256,2048]{1,0:T(8,128)}, f32[256,2048]{1,0:T(8,128)}, f32[256,2048]{1,0:T(8,128)}) fusion(f32[256,2048]{1,0:T(8,128)S(1)} %copy-done, f32[256,2048]{1,0:T(8,128)S(1)} %get-tuple-element.7, f32[256,2048]{1,0:T(8,128)S(1)} %copy-done.1, f32[256,2048]{1,0:T(8,128)S(1)} %copy-done.2), kind=kLoop, calls=%fused_computation.2 | loop fusion | flops 7864320 | bytes 14680064 | tf_op jit(solution)/shard_map/sub | solution.py:40
  110.3 1.0 copy.12
Async XLA Ops:
  0.6 105.6 %copy-start = (f32[256,2048]{1,0:T(8,128)S(1)}, f32[256,2048]{1,0:T(8,128)}, u32[]{:S(2)}) copy-start(f32[256,2048]{1,0:T(8,128)} %param.11) | copy-start | bytes 6291460
  0.6 105.6 %copy-start.1 = (f32[256,2048]{1,0:T(8,128)S(1)}, f32[256,2048]{1,0:T(8,128)}, u32[]{:S(2)}) copy-start(f32[256,2048]{1,0:T(8,128)} %param.12) | copy-start | bytes 6291460
  0.7 105.6 %copy-start.2 = (f32[256,2048]{1,0:T(8,128)S(1)}, f32[256,2048]{1,0:T(8,128)}, u32[]{:S(2)}) copy-start(f32[256,2048]{1,0:T(8,128)} %param.13) | copy-start | bytes 6291460
where the time goes:
time: 111 us
  Pallas kernels  106 us (95%)
  other arithmetic  4.03 us (4%)
    pallas_call x1, Pallas kernels, fused(): pl.pallas_call(functools.partial(kernel, Z, G), out_shape=(jax.ShapeDtype...  106 us
    sub x1, other arithmetic, adamw(): new_master = master - LEARN_RATE * (update + DECAY_RATE * master)  4.03 us

commit v1 on v0

--- a/solution.py
+++ b/solution.py
@@ -18,8 +18,9 @@
 EPS_NORM = 1e-06
 
 MESH = pl.DeviceIdType.MESH
-PIECES = 4
-DEPTH = 3
+PIECES = 8
+SIDES = 2
+DEPTH = 5
 
 
 def dequantize(codes, scales):
@@ -36,7 +37,9 @@
     new_moment_two = BETA_TWO * moment_two + (1.0 - BETA_TWO) * clipped * clipped
     first_fix = 1.0 - BETA_ONE**10
     second_fix = 1.0 - BETA_TWO**10
-    update = new_moment_one / first_fix / (jnp.sqrt(new_moment_two / second_fix) + EPS_ADAM)
+    update = (new_moment_one * (1.0 / first_fix)) / (
+        jnp.sqrt(new_moment_two * (1.0 / second_fix)) + EPS_ADAM
+    )
     new_master = master - LEARN_RATE * (update + DECAY_RATE * master)
     return new_master, new_moment_one, new_moment_two
 
@@ -75,7 +78,7 @@
     feat, cols = codes_ref.shape
     half = cols // 2
     unit = 2 * feat
-    g_rows, r_rows = feat // K, unit // K
+    g_rows, r_rows, r_cols = feat // K, unit // (K // SIDES), half // SIDES
 
     dp, g = lax.axis_index("dp"), lax.axis_index("group")
     z = lax.div(dp, 2)
@@ -162,8 +165,14 @@
     def weight_chunk(zz, core, k):
         return wbuf.at[pl.ds(pl.multiple_of((2 * zz + core) * feat + k * g_rows, g_rows), g_rows), :]
 
+    def span(k):
+        row = lax.div(k, SIDES)
+        col = k - row * SIDES
+        return (pl.ds(pl.multiple_of(row * r_rows, r_rows), r_rows),
+                pl.ds(pl.multiple_of(col * r_cols, r_cols), r_cols))
+
     def sum_chunk(way, dm, k):
-        return rbuf.at[way, dm - 1, pl.ds(pl.multiple_of(k * r_rows, r_rows), r_rows), :]
+        return rbuf.at[(way, dm - 1) + span(k)]
 
     def line_copy(way, ref, step):
         return remote(ref, ref, line_send.at[way, step], line_recv.at[way, step], nexts[way])
@@ -173,9 +182,9 @@
         return remote(ref, ref, sib_send.at[zz * K + k], sib_recv.at[zz * K + k], sibling)
 
     def partial_sum(zz, k):
-        first = pl.multiple_of(zz * unit + k * r_rows, r_rows)
+        first = pl.multiple_of(zz * unit + lax.div(k, SIDES) * r_rows, r_rows)
         return lax.dot_general(
-            cotp[:, pl.ds(first, r_rows)], lip[...],
+            cotp[:, pl.ds(first, r_rows)], lip[:, span(k)[1]],
             (((0,), (0,)), ((), ())), preferred_element_type=jnp.float32,
         )
 
@@ -270,22 +279,21 @@
     lax.fori_loop(0, cols // BLOCK, input_tile, 0)
 
     def own_sum(k, carry):
-        facc[pl.ds(pl.multiple_of(k * r_rows, r_rows), r_rows), :] = partial_sum(z, k)
+        facc[span(k)] = partial_sum(z, k)
         return carry
 
     lax.fori_loop(0, K, own_sum, 0)
 
     def fin_copy(k, m):
         return remote(
-            facc.at[pl.ds(pl.multiple_of(k * r_rows, r_rows), r_rows), :],
-            gsib.at[pl.ds(pl.multiple_of(m * r_rows, r_rows), r_rows), :],
+            facc.at[span(k)], gsib.at[span(m)],
             fin_send.at[m], fin_recv.at[m], sibling,
         )
 
     near[0] = jnp.zeros(near.shape[1:], jnp.float32)
 
     def finish(k, carry):
-        at = pl.ds(pl.multiple_of(k * r_rows, r_rows), r_rows)
+        at = span(k)
         for way in (0, 1):
             p = places[way]
 
@@ -293,7 +301,7 @@
             def _():
                 ref = sum_chunk(way, p, k)
                 line_copy(way, ref, (Z - 1) * K + k).wait_recv()
-                facc[at, :] += ref[...].astype(jnp.float32)
+                facc[at] += ref[...].astype(jnp.float32)
 
         core = lax.div(k, K // 2)
 
@@ -301,13 +309,13 @@
         def _():
             fin_copy(k, k - core * (K // 2)).start()
 
-        value = facc[at, :]
+        value = facc[at]
         squares = value * value
         total = squares[0:8, :]
         for i in range(1, r_rows // 8):
             total = total + squares[i * 8:(i + 1) * 8, :]
         short = total[:, 0:128]
-        for i in range(1, half // 128):
+        for i in range(1, r_cols // 128):
             short = short + total[:, i * 128:(i + 1) * 128]
         near[0] += short
         return carry

time: 111 us -> 112 us (level)
  no operation moved by 1% of the time
where the time goes in v1:
time: 112 us
  Pallas kernels  107 us (96%)
  other arithmetic  4.03 us (4%)
    pallas_call x1, Pallas kernels, fused(): pl.pallas_call(functools.partial(kernel, Z, G), out_shape=(jax.ShapeDtype...  107 us
    sub x1, other arithmetic, adamw(): new_master = master - LEARN_RATE * (update + DECAY_RATE * master)  4.03 us

profile of v1, /device:TPU:0, one launch (start us, length us, event | category | flops | bytes accessed | tf_op | source)
XLA Modules:
  0.0 112.3 jit_solution(18135987514252022004)
XLA Ops:
  0.6 0.0 copy-start
  0.6 0.0 copy-start.1
  0.7 0.0 copy-start.2
  0.7 106.6 %shard_map.102 = (bf16[256,2048]{1,0:T(8,128)(2,1)S(1)}, f32[256,2048]{1,0:T(8,128)S(1)}) custom-call(bf16[256,512]{1,0:T(8,128)(2,1)} %cot_ref.1, bf16[256,2048]{1,0:T(8,128)(2,1)} %li_ref.1, bf16[256,2048]{1,0:T(8,128)(2,1)} %codes_ref.1, bf16[8,256]{1,0:T(8,128)(2,1)} %bitcast.1), custom_call_target="tpu_custom_call" | custom-call | flops 4294967296 | bytes 5242880 | tf_op jit(solution)/shard_map/pallas_call | solution.py:382
  107.3 0.0 copy-done
  107.3 0.0 copy-done.1
  107.3 0.0 copy-done.2
  107.3 4.0 %multiply_subtract_fusion = (f32[256,2048]{1,0:T(8,128)}, f32[256,2048]{1,0:T(8,128)}, f32[256,2048]{1,0:T(8,128)}) fusion(f32[256,2048]{1,0:T(8,128)S(1)} %copy-done, f32[256,2048]{1,0:T(8,128)S(1)} %get-tuple-element.7, f32[256,2048]{1,0:T(8,128)S(1)} %copy-done.1, f32[256,2048]{1,0:T(8,128)S(1)} %copy-done.2), kind=kLoop, calls=%fused_computation.2 | loop fusion | flops 7864320 | bytes 14680064 | tf_op jit(solution)/shard_map/sub | solution.py:43
  111.3 1.0 copy.12
Async XLA Ops:
  0.6 106.6 %copy-start = (f32[256,2048]{1,0:T(8,128)S(1)}, f32[256,2048]{1,0:T(8,128)}, u32[]{:S(2)}) copy-start(f32[256,2048]{1,0:T(8,128)} %param.11) | copy-start | bytes 6291460
  0.6 106.6 %copy-start.1 = (f32[256,2048]{1,0:T(8,128)S(1)}, f32[256,2048]{1,0:T(8,128)}, u32[]{:S(2)}) copy-start(f32[256,2048]{1,0:T(8,128)} %param.12) | copy-start | bytes 6291460
  0.7 106.6 %copy-start.2 = (f32[256,2048]{1,0:T(8,128)S(1)}, f32[256,2048]{1,0:T(8,128)}, u32[]{:S(2)}) copy-start(f32[256,2048]{1,0:T(8,128)} %param.13) | copy-start | bytes 6291460

commit v2 on v0

--- a/solution.py
+++ b/solution.py
@@ -19,7 +19,7 @@
 
 MESH = pl.DeviceIdType.MESH
 PIECES = 4
-DEPTH = 3
+DEPTH = 2
 
 
 def dequantize(codes, scales):

time: 111 us -> 113 us (1.018)
    pallas_call x1, Pallas kernels: 106 us -> 107 us  [fused(): pl.pallas_call(functools.partial(kernel, Z, G), out_shape=(jax.ShapeDtype...]
where the time goes in v2:
time: 113 us
  Pallas kernels  107 us (95%)
  other arithmetic  4.03 us (4%)
    pallas_call x1, Pallas kernels, fused(): pl.pallas_call(functools.partial(kernel, Z, G), out_shape=(jax.ShapeDtype...  107 us
    sub x1, other arithmetic, adamw(): new_master = master - LEARN_RATE * (update + DECAY_RATE * master)  4.03 us

profile of v2, /device:TPU:0, one launch (start us, length us, event | category | flops | bytes accessed | tf_op | source)
XLA Modules:
  0.0 113.2 jit_solution(11303822424070355656)
XLA Ops:
  0.6 0.0 copy-start
  0.6 0.0 copy-start.1
  0.7 0.0 copy-start.2
  0.7 107.5 %shard_map.102 = (bf16[256,2048]{1,0:T(8,128)(2,1)S(1)}, f32[256,2048]{1,0:T(8,128)S(1)}) custom-call(bf16[256,512]{1,0:T(8,128)(2,1)} %cot_ref.1, bf16[256,2048]{1,0:T(8,128)(2,1)} %li_ref.1, bf16[256,2048]{1,0:T(8,128)(2,1)} %codes_ref.1, bf16[8,256]{1,0:T(8,128)(2,1)} %bitcast.1), custom_call_target="tpu_custom_call" | custom-call | flops 4294967296 | bytes 5242880 | tf_op jit(solution)/shard_map/pallas_call | solution.py:374
  108.2 0.0 copy-done
  108.2 0.0 copy-done.1
  108.2 0.0 copy-done.2
  108.2 4.0 %multiply_subtract_fusion = (f32[256,2048]{1,0:T(8,128)}, f32[256,2048]{1,0:T(8,128)}, f32[256,2048]{1,0:T(8,128)}) fusion(f32[256,2048]{1,0:T(8,128)S(1)} %copy-done, f32[256,2048]{1,0:T(8,128)S(1)} %get-tuple-element.7, f32[256,2048]{1,0:T(8,128)S(1)} %copy-done.1, f32[256,2048]{1,0:T(8,128)S(1)} %copy-done.2), kind=kLoop, calls=%fused_computation.2 | loop fusion | flops 7864320 | bytes 14680064 | tf_op jit(solution)/shard_map/sub | solution.py:40
  112.2 1.0 copy.12
Async XLA Ops:
  0.6 107.5 %copy-start = (f32[256,2048]{1,0:T(8,128)S(1)}, f32[256,2048]{1,0:T(8,128)}, u32[]{:S(2)}) copy-start(f32[256,2048]{1,0:T(8,128)} %param.11) | copy-start | bytes 6291460
  0.6 107.5 %copy-start.1 = (f32[256,2048]{1,0:T(8,128)S(1)}, f32[256,2048]{1,0:T(8,128)}, u32[]{:S(2)}) copy-start(f32[256,2048]{1,0:T(8,128)} %param.12) | copy-start | bytes 6291460
  0.7 107.5 %copy-start.2 = (f32[256,2048]{1,0:T(8,128)S(1)}, f32[256,2048]{1,0:T(8,128)}, u32[]{:S(2)}) copy-start(f32[256,2048]{1,0:T(8,128)} %param.13) | copy-start | bytes 6291460
